TPU v7x, 32 devices: a whole 2x2x4 slice. The times are simulated.
32 devices in a mesh: feat: 4 (over x, core), work: 8 (over z, y).
Axes of the slice: x: 2, y: 2, z: 4, core: 2. Of those that a mesh axis runs over, the one named last changes fastest.
Arguments:
- momentum: bfloat16 [8, 8192, 1024], P('work', 'feat'), may hold values from -6 to 6
- gradient: bfloat16 [8, 8192, 1024], P('work', 'feat'), may hold values from -6 to 6
- weight: bfloat16 [8192, 1024], P('feat'), may hold values from -3 to 3
- tokens: bfloat16 [8192, 8192], P('work', 'feat'), may hold values from -6 to 6
- select: int32 [8, 64, 8, 4], P('work', 'feat'), may hold values from 0 to 127, as said below
Outputs:
- moment_out: bfloat16 [8, 8192, 1024], P('work', 'feat')
- weight_out: bfloat16 [8192, 1024], P('feat')
- projected: bfloat16 [8192, 1024], P('work', 'feat')
Inputs may be any that keep to these rules, and one draw needn't show every extreme that they name: `select`: for each worker and tile the 4 indices are distinct.
All inputs are finite; a program needn't handle non-finite values.
Results may differ from a plain program's by a relative error of at most 0.015.
Values may be sent and summed in bfloat16 or wider, within the bound.
A program may use at most 128 MiB of HBM per device.

v0:
```python
import math
import jax
import jax.numpy as jnp
from jax import lax
from jax.sharding import PartitionSpec as P

D = 8192
TILE = 128
HIGHEST_PRECISION = lax.Precision.HIGHEST
DECAY = 0.9
RATE = 8.0


def cosine_basis(order):
    freq = jnp.arange(order, dtype=jnp.int32).astype(jnp.float32)[:, None]
    place = jnp.arange(order, dtype=jnp.int32).astype(jnp.float32)[None, :]
    scale = jnp.where(freq == 0.0, math.sqrt(1.0 / order), math.sqrt(2.0 / order))
    return scale * jnp.cos(math.pi * (2.0 * place + 1.0) * freq / (2.0 * order))


def local(momentum, gradient, weight, tokens, select):
    transform = cosine_basis(TILE)
    local_rows, out_width = weight.shape
    row_tiles = local_rows // TILE
    col_tiles = out_width // TILE
    workers = lax.axis_size("work")
    positions = jnp.arange(TILE, dtype=jnp.int32)
    chosen = select[0]
    blended = (DECAY * momentum[0].astype(jnp.float32) + gradient[0].astype(jnp.float32)).reshape(
        row_tiles, TILE, col_tiles, TILE
    )
    onehot = (chosen[..., None] == positions).astype(jnp.float32)
    rows_basis = jnp.einsum("abkr,rj->abkj", onehot, transform, precision=HIGHEST_PRECISION)
    partial_value = jnp.einsum("abkr,arbc->akbc", rows_basis, blended, precision=HIGHEST_PRECISION)
    decoded = jnp.einsum("abkr,akbc->arbc", rows_basis, partial_value, precision=HIGHEST_PRECISION)
    moment_out = (blended - decoded).reshape(local_rows, out_width).astype(jnp.bfloat16)[None]
    row_marks = jnp.arange(TILE, dtype=jnp.int32).astype(jnp.float32)
    initial = jnp.zeros((row_tiles, TILE, col_tiles, TILE), jnp.float32)
    values = lax.all_gather(
        partial_value[None].astype(jnp.bfloat16), "work", axis=0, tiled=True
    ).astype(jnp.float32)
    locations = lax.all_gather(
        chosen.astype(jnp.float32)[None].astype(jnp.bfloat16), "work", axis=0, tiled=True
    ).astype(jnp.float32)
    indicator = (locations[..., None] == row_marks).astype(jnp.float32)
    summed = initial + jnp.einsum(
        "nabkr,nakbc->arbc", indicator, values, precision=HIGHEST_PRECISION
    )
    weight_out = (
        weight.astype(jnp.float32)
        - RATE
        * jnp.einsum(
            "rj,arbc->ajbc", transform, summed / workers, precision=HIGHEST_PRECISION
        ).reshape(local_rows, out_width)
    ).astype(jnp.bfloat16)
    summed_out = lax.psum_scatter(
        lax.dot_general(
            weight_out, tokens, (((0,), (1,)), ((), ())), preferred_element_type=jnp.float32
        ).astype(jnp.bfloat16),
        "feat",
        scatter_dimension=0,
        tiled=True,
    ).astype(jnp.float32)
    projected = (summed_out.T * (1.0 / math.sqrt(D))).astype(jnp.bfloat16)
    return (moment_out, weight_out, projected)


def solution(mesh):
    in_specs = (
        P("work", "feat", None),
        P("work", "feat", None),
        P("feat", None),
        P("work", "feat"),
        P("work", "feat", None, None),
    )
    out_specs = (P("work", "feat", None), P("feat", None), P("work", "feat"))
    return jax.shard_map(local, mesh=mesh, in_specs=in_specs, out_specs=out_specs, check_vma=False)
```

profile of v0, /device:TPU:0, one launch (start us, length us, event | category | flops | bytes accessed | tf_op | source)
XLA Modules:
  0.0 166.0 jit_solution(15831966459224031147)
XLA Ops:
  7.2 0.0 all-gather.3.cloned.1.call-start
  7.2 0.8 copy.35
  8.0 0.1 iota_compare_fusion
  8.2 5.5 %add_bitcast_fusion = f32[256,8,8,128]{3,1,2,0:T(8,128)S(1)} fusion(bf16[1,2048,1024]{2,1,0:T(8,128)(2,1)} %param.6, bf16[1,2048,1024]{2,1,0:T(8,128)(2,1)} %param.5), kind=kLoop, calls=%fused_computation.8 | loop fusion | flops 8388608 | bytes 16777216
  13.7 5.3 %copy.54 = f32[256,8,8,128]{3,2,1,0:T(8,128)} copy(f32[256,8,8,128]{3,1,2,0:T(8,128)S(1)} %add_bitcast_fusion) | data formatting | bytes 16777216
  19.0 9.3 %copy.39 = f32[16,128,8,128]{1,3,2,0:T(8,128)} copy(f32[16,128,8,128]{3,2,1,0:T(8,128)} %bitcast.51) | data formatting | bytes 16777216 | tf_op jit(solution)/shard_map/add | solution.py:29
  28.3 0.0 copy-start.1
  28.3 0.6 fusion.11
  28.9 15.4 %fusion.27 = (bf16[16,4,8,128]{3,1,2,0:T(4,128)(2,1)S(1)}, f32[16,4,8,128]{3,1,2,0:T(4,128)S(1)}) fusion(f32[16,128,8,128]{1,3,2,0:T(8,128)} %copy.39, f32[16,8,4,128]{3,2,1,0:T(4,128)S(1)} %fusion.11), kind=kOutput, calls=%fused_computation.40 | convolution fusion | flops 100728832 | bytes 9043968 | tf_op jit(solution)/shard_map/abkr,arbc->akbc/dot_general | solution.py:34
  44.2 0.7 copy.41
  44.9 0.0 all-gather.3.cloned.1.call-update
  45.0 0.0 reduce-scatter.2.cloned.1.call-start
  45.0 0.0 copy-done.1
  45.0 32.6 %all_gather.7 = bf16[8,16,8,4]{1,2,3,0:T(8,128)(2,1)S(1)} all-gather(bf16[1,16,8,4]{1,2,3,0:T(8,128)(2,1)S(1)} %fusion.23), channel_id=1, replica_groups=mesh['feat'=4,'work'=8] {'work'}, dimensions={0}, use_global_device_ids=true | all-gather | bytes 9216 | tf_op jit(solution)/shard_map/all_gather | solution.py:42
  77.7 0.5 copy.43
  78.2 9.9 %all-gather.3.cloned.1.call-done = bf16[128,4,8,128]{3,2,1,0:T(8,128)(2,1)} async-done(((bf16[16,4,8,128]{3,2,1,0:T(8,128)(2,1)}), bf16[128,4,8,128]{3,2,1,0:T(8,128)(2,1)}) %all-gather.3.cloned.1.call-update) | async-done | bytes 1048592 | tf_op jit(solution)/shard_map/all_gather | solution.py:39
  88.1 4.8 %fusion.7 = f32[16,8,128,128,1]{3,2,4,1,0:T(8,128)S(1)} fusion(bf16[8,16,4,8,128]{4,3,2,1,0:T(8,128)(2,1)} %bitcast.54, f32[128]{0:T(128)S(1)} %iota_convert_fusion, f32[8,16,8,4]{3,2,1,0:T(8,128)S(1)} %copy.43), kind=kOutput, calls=%fused_computation.10 | convolution fusion | flops 134742016 | bytes 9454080 | tf_op jit(solution)/shard_map/nabkr,nakbc->arbc/dot_general | solution.py:46
  92.9 9.5 %multiply_bitcast_fusion = f32[16,128,8,128]{1,3,2,0:T(8,128)} fusion(f32[16,8,128,128,1]{3,2,4,1,0:T(8,128)S(1)} %fusion.7, f32[128]{0:T(128)S(1)} %iota_convert_fusion, f32[128]{0:T(128)S(1)} %get-tuple-element.18, f32[128]{0:T(128)S(1)} %get-tuple-element.17), kind=kOutput, calls=%fused_computation.7 | convolution fusion | flops 3225468928 | bytes 16778752 | tf_op jit(solution)/shard_map/rj,arbc->ajbc/dot_general | solution.py:52
  102.4 9.3 %copy.45 = f32[16,128,8,128]{3,2,1,0:T(8,128)} copy(f32[16,128,8,128]{1,3,2,0:T(8,128)} %multiply_bitcast_fusion) | data formatting | bytes 16777216 | tf_op jit(solution)/shard_map/mul | solution.py:51
  111.6 0.0 copy-start.2
  111.6 6.9 %fusion = bf16[2048,1024]{1,0:T(8,128)(2,1)S(1)} fusion(f32[256,8,8,128]{3,2,1,0:T(8,128)} %bitcast.52, bf16[2048,1024]{1,0:T(8,128)(2,1)} %param.7), kind=kLoop, calls=%fused_computation.1 | loop fusion | flops 6291456 | bytes 16777216 | tf_op jit(solution)/shard_map/convert_element_type | solution.py:55
  118.6 0.0 copy-start
  118.6 2.0 %copy-done = bf16[2048,1024]{1,0:T(8,128)(2,1)} copy-done((bf16[2048,1024]{1,0:T(8,128)(2,1)}, bf16[2048,1024]{1,0:T(8,128)(2,1)S(1)}, u32[]{:S(2)}) %copy-start) | copy-done | bytes 4194328
  120.6 0.0 copy-done.2
  120.6 5.8 %convolution_convert_fusion = bf16[1024,1024]{1,0:T(8,128)(2,1)} fusion(bf16[2048,1024]{1,0:T(8,128)(2,1)S(1)} %fusion, bf16[1024,2048]{1,0:T(8,128)(2,1)S(1)} %copy-done.2), kind=kOutput, calls=%fused_computation.12 | convolution fusion | flops 4296015872 | bytes 10485760 | tf_op jit(solution)/shard_map/dot_general | solution.py:57
  126.4 0.0 reduce-scatter.2.cloned.1.call-update
  126.4 16.6 %fusion.3 = bf16[16,128,8,128]{1,3,2,0:T(8,128)(2,1)} fusion(f32[16,128,8,128]{1,3,2,0:T(8,128)} %copy.39, f32[16,4,8,128]{3,1,2,0:T(4,128)S(1)} %get-tuple-element.16, f32[16,8,4,128]{3,2,1,0:T(4,128)S(1)} %fusion.11), kind=kOutput, calls=%fused_computation.6 | convolution fusion | flops 104857600 | bytes 13107200 | tf_op jit(solution)/shard_map/abkr,akbc->arbc/dot_general | solution.py:35
  143.0 6.7 %copy.40 = bf16[16,128,8,128]{3,2,1,0:T(8,128)(2,1)} copy(bf16[16,128,8,128]{1,3,2,0:T(8,128)(2,1)} %fusion.3) | data formatting | bytes 8388608 | tf_op jit(solution)/shard_map/convert_element_type | solution.py:36
  149.7 7.3 %convert_element_type.90 = bf16[1,2048,1024]{2,1,0:T(8,128)(2,1)} reshape(bf16[16,128,8,128]{3,2,1,0:T(8,128)(2,1)} %copy.40) | data formatting | bytes 8388608 | tf_op jit(solution)/shard_map/convert_element_type | solution.py:36
  157.0 0.0 reduce-scatter.2.cloned.1.call-done
  157.0 1.1 fusion.10
  158.1 1.0 copy.46
  (3 shorter events, 0.0 us)
Async XLA Ops:
  7.2 80.9 %all-gather.3.cloned.1.call-start = ((), (), s32[]{:S(2)}) async-start(), calls=%async_computation.2 | async-start | bytes 1179648 | tf_op jit(solution)/shard_map/all_gather | solution.py:39
  28.3 16.8 %copy-start.1 = (s32[1,16,8,4]{1,3,2,0:T(4,128)S(1)}, s32[1,16,8,4]{1,3,2,0:T(4,128)}, u32[]{:S(2)}) copy-start(s32[1,16,8,4]{1,3,2,0:T(4,128)} %param.9) | copy-start | bytes 6148
  45.0 112.0 %reduce-scatter.2.cloned.1.call-start = ((), (), s32[]{:S(2)}) async-start(), calls=%async_computation.1 | async-start | bytes 2621440 | tf_op jit(solution)/shard_map/reduce_scatter | solution.py:56
  111.6 9.0 %copy-start.2 = (bf16[1024,2048]{1,0:T(8,128)(2,1)S(1)}, bf16[1024,2048]{1,0:T(8,128)(2,1)}, u32[]{:S(2)}) copy-start(bf16[1024,2048]{1,0:T(8,128)(2,1)} %param.8) | copy-start | bytes 12582916
  118.6 2.0 %copy-start = (bf16[2048,1024]{1,0:T(8,128)(2,1)}, bf16[2048,1024]{1,0:T(8,128)(2,1)S(1)}, u32[]{:S(2)}) copy-start(bf16[2048,1024]{1,0:T(8,128)(2,1)S(1)} %fusion) | copy-start | bytes 12582916
Sparse Core Ops, SparseCore 0:
  45.1 42.9 all-gather.2
  126.5 30.2 reduce-scatter.1
where the time goes:
time: 167 us; the launch traced here: 166 us
  matrix products  52.6 us (31%)
  local copies, waits for them, and re-layouts  42.9 us (26%)
  blocking collectives  32.6 us (20%)
  between operations  14.1 us (8%)
  other arithmetic  13.7 us (8%)
  waiting for transfers between devices  9.98 us (6%)
    all_gather x1, blocking collectives, local(): lax.all_gather(chosen.astype(jnp.float32)[None].astype(jnp.bfloat16), 'wo...  32.6 us
    dot_general x1, matrix products, local(): jnp.einsum('abkr,akbc->arbc', rows_basis, partial_value, precision=HIGHES...  16.6 us
    dot_general x1, matrix products, local(): jnp.einsum('abkr,arbc->akbc', rows_basis, blended, precision=HIGHEST_PREC...  15.4 us
    convert_element_type x2, local copies, waits for them, and re-layouts, local(): (blended - decoded).reshape(local_rows, out_width).astype(jnp.bfloat16)  14 us
    all_gather x1, waiting for transfers between devices, local(): lax.all_gather(partial_value[None].astype(jnp.bfloat16), 'work', axis=0,...  9.95 us
    dot_general x1, matrix products, local(): jnp.einsum('rj,arbc->ajbc', transform, summed / workers, precision=HIGHES...  9.49 us
    add x1, local copies, waits for them, and re-layouts, local(): DECAY * momentum[0].astype(jnp.float32) + gradient[0].astype(jnp.float32)  9.29 us
    mul x1, local copies, waits for them, and re-layouts, local(): RATE * jnp.einsum('rj,arbc->ajbc', transform, summed / workers, precision...  9.28 us
  transfers between devices with their start and end apart: 2, of which 1 were waited for; matrix products, arithmetic and copies ran while one was open for 19% of the time, Pallas kernels for 0%

commit v1 on v0

--- a/solution.py
+++ b/solution.py
@@ -9,6 +9,22 @@
 HIGHEST_PRECISION = lax.Precision.HIGHEST
 DECAY = 0.9
 RATE = 8.0
+
+
+def collect(x, axis, dim):
+    ways, here, step = (lax.axis_size(axis), lax.axis_index(axis), x.shape[dim])
+    dims = [n * ways if d == dim else n for d, n in enumerate(x.shape)]
+    full = lax.dynamic_update_slice_in_dim(jnp.zeros(dims, x.dtype), x, here * step, axis=dim)
+    going_up = going_down = x
+    for far in range(1, ways // 2 + 1):
+        going_up = lax.ppermute(going_up, axis, [(d, (d + 1) % ways) for d in range(ways)])
+        full = lax.dynamic_update_slice_in_dim(full, going_up, (here - far) % ways * step, axis=dim)
+        if 2 * far < ways:
+            going_down = lax.ppermute(going_down, axis, [(d, (d - 1) % ways) for d in range(ways)])
+            full = lax.dynamic_update_slice_in_dim(
+                full, going_down, (here + far) % ways * step, axis=dim
+            )
+    return full
 
 
 def cosine_basis(order):
@@ -36,9 +52,7 @@
     moment_out = (blended - decoded).reshape(local_rows, out_width).astype(jnp.bfloat16)[None]
     row_marks = jnp.arange(TILE, dtype=jnp.int32).astype(jnp.float32)
     initial = jnp.zeros((row_tiles, TILE, col_tiles, TILE), jnp.float32)
-    values = lax.all_gather(
-        partial_value[None].astype(jnp.bfloat16), "work", axis=0, tiled=True
-    ).astype(jnp.float32)
+    values = collect(partial_value[None].astype(jnp.bfloat16), "work", 0).astype(jnp.float32)
     locations = lax.all_gather(
         chosen.astype(jnp.float32)[None].astype(jnp.bfloat16), "work", axis=0, tiled=True
     ).astype(jnp.float32)

time: 167 us -> 182 us (1.090)
  starting transfers between devices: 0.08 us -> 15.6 us
  waiting for transfers between devices: 9.98 us -> 13.7 us
  blocking collectives: 32.6 us -> 30.5 us
  matrix products: 52.6 us -> 50.7 us
    ppermute x0 -> x7, starting transfers between devices: none -> 15.6 us  [the longest x3 12.5 us: collect(): lax.ppermute(going_down, axis, [(d, (d - 1) % ways) for d in range(ways)])]
    ppermute x0 -> x7, waiting for transfers between devices: none -> 13.7 us  [the longest x4 13.6 us: collect(): lax.ppermute(going_up, axis, [(d, (d + 1) % ways) for d in range(ways)])]
    all_gather x1 -> x0, waiting for transfers between devices: 9.95 us -> none  [local(): lax.all_gather(partial_value[None].astype(jnp.bfloat16), 'work', axis=0,...]
    all_gather x1, blocking collectives: 32.6 us -> 30.5 us  [local(): lax.all_gather(chosen.astype(jnp.float32)[None].astype(jnp.bfloat16), 'wo...]
  transfers between devices with their start and end apart: 2 -> 8, of which waited for: 1 -> 3; matrix products, arithmetic and copies ran while one was open for 19% -> 18% of each run, Pallas kernels for 0% -> 0%
where the time goes in v1:
time: 182 us
  matrix products  50.7 us (28%)
  local copies, waits for them, and re-layouts  43.1 us (24%)
  blocking collectives  30.5 us (17%)
  starting transfers between devices  15.6 us (9%)
  between operations  14.2 us (8%)
  other arithmetic  13.8 us (8%)
  waiting for transfers between devices  13.7 us (8%)
    all_gather x1, blocking collectives, local(): lax.all_gather(chosen.astype(jnp.float32)[None].astype(jnp.bfloat16), 'wo...  30.5 us
    dot_general x1, matrix products, local(): jnp.einsum('abkr,akbc->arbc', rows_basis, partial_value, precision=HIGHES...  16.6 us
    dot_general x1, matrix products, local(): jnp.einsum('abkr,arbc->akbc', rows_basis, blended, precision=HIGHEST_PREC...  15.4 us
    convert_element_type x2, local copies, waits for them, and re-layouts, local(): (blended - decoded).reshape(local_rows, out_width).astype(jnp.bfloat16)  14 us
    ppermute x4, waiting for transfers between devices, collect(): lax.ppermute(going_up, axis, [(d, (d + 1) % ways) for d in range(ways)])  13.6 us
    ppermute x3, starting transfers between devices, collect(): lax.ppermute(going_down, axis, [(d, (d - 1) % ways) for d in range(ways)])  12.5 us
    dot_general x1, matrix products, local(): jnp.einsum('rj,arbc->ajbc', transform, summed / workers, precision=HIGHES...  9.41 us
    add x1, local copies, waits for them, and re-layouts, local(): DECAY * momentum[0].astype(jnp.float32) + gradient[0].astype(jnp.float32)  9.28 us
  transfers between devices with their start and end apart: 8, of which 3 were waited for; matrix products, arithmetic and copies ran while one was open for 18% of the time, Pallas kernels for 0%

profile of v1, /device:TPU:0, one launch (start us, length us, event | category | flops | bytes accessed | tf_op | source)
XLA Modules:
  0.0 181.6 jit_solution(4495020270984684807)
XLA Ops:
  7.2 0.8 copy.23
  8.0 0.1 iota_compare_fusion
  8.2 5.5 %add_bitcast_fusion = f32[256,8,8,128]{3,1,2,0:T(8,128)S(1)} fusion(bf16[1,2048,1024]{2,1,0:T(8,128)(2,1)} %param.6, bf16[1,2048,1024]{2,1,0:T(8,128)(2,1)} %param.5), kind=kLoop, calls=%fused_computation.9 | loop fusion | flops 8388608 | bytes 16777216
  13.7 5.3 %copy.48 = f32[256,8,8,128]{3,2,1,0:T(8,128)} copy(f32[256,8,8,128]{3,1,2,0:T(8,128)S(1)} %add_bitcast_fusion) | data formatting | bytes 16777216
  19.0 9.3 %copy.27 = f32[16,128,8,128]{1,3,2,0:T(8,128)} copy(f32[16,128,8,128]{3,2,1,0:T(8,128)} %bitcast.50) | data formatting | bytes 16777216 | tf_op jit(solution)/shard_map/add | solution.py:45
  28.3 0.6 fusion.11
  28.9 15.4 %convolution_bitcast_fusion = f32[16,4,8,128]{3,1,2,0:T(4,128)S(1)} fusion(f32[16,128,8,128]{1,3,2,0:T(8,128)} %copy.27, f32[16,8,4,128]{3,2,1,0:T(4,128)S(1)} %fusion.11), kind=kOutput, calls=%fused_computation.13 | convolution fusion | flops 100663296 | bytes 8912896 | tf_op jit(solution)/shard_map/abkr,arbc->akbc/dot_general | solution.py:50
  44.3 3.0 %collective-permute-start = (bf16[1,16,4,8,128]{4,2,3,1,0:T(4,128)(2,1)S(1)}, bf16[1,16,4,8,128]{4,2,3,1,0:T(4,128)(2,1)S(1)}, u32[]{:S(2)}, u32[]{:S(2)}) collective-permute-start(bf16[1,16,4,8,128]{4,2,3,1,0:T(4,128)(2,1)S(1)} %convert_bitcast_fusion), channel_id=1, source_target_pairs={{0,1},{1,2},{2,3},{3,4},{4,5},{5,6},{6,7},{7,0},{8,9},{9,10},{10,1... | collective-permute-start | bytes 393224 | tf_op jit(solution)/shard_map/ppermute | solution.py:20
  47.3 3.1 %collective-permute-start.1 = (bf16[1,16,4,8,128]{4,2,3,1,0:T(4,128)(2,1)S(1)}, bf16[1,16,4,8,128]{4,2,3,1,0:T(4,128)(2,1)S(1)}, u32[]{:S(2)}, u32[]{:S(2)}) collective-permute-start(bf16[1,16,4,8,128]{4,2,3,1,0:T(4,128)(2,1)S(1)} %convert_bitcast_fusion), channel_id=1, source_target_pairs={{0,7},{1,0},{2,1},{3,2},{4,3},{5,4},{6,5},{7,6},{8,15},{9,8},{10,9... | collective-permute-start | bytes 393224 | tf_op jit(solution)/shard_map/ppermute | solution.py:23
  50.4 30.5 %all_gather.3 = bf16[8,16,8,4]{1,2,3,0:T(8,128)(2,1)S(1)} all-gather(bf16[1,16,8,4]{1,2,3,0:T(8,128)(2,1)S(1)} %fusion.23), channel_id=1, replica_groups=mesh['feat'=4,'work'=8] {'work'}, dimensions={0}, use_global_device_ids=true | all-gather | bytes 9216 | tf_op jit(solution)/shard_map/all_gather | solution.py:56
  80.9 0.5 copy.38
  81.4 0.5 broadcast_in_dim.12
  82.1 4.7 %collective-permute-start.3 = (bf16[1,16,4,8,128]{4,2,3,1,0:T(4,128)(2,1)S(1)}, bf16[1,16,4,8,128]{4,2,3,1,0:T(4,128)(2,1)S(1)}, u32[]{:S(2)}, u32[]{:S(2)}) collective-permute-start(bf16[1,16,4,8,128]{4,2,3,1,0:T(4,128)(2,1)S(1)} %collective-permute-done.1), channel_id=1, source_target_pairs={{0,7},{1,0},{2,1},{3,2},{4,3},{5,4},{6,5},{7,6},{8,15},{9,8},{10,9... | collective-permute-start | bytes 393224 | tf_op jit(solution)/shard_map/ppermute | solution.py:23
  86.8 0.1 copy_dynamic-update-slice_fusion.5
  86.9 3.2 %collective-permute-done.2 = bf16[1,16,4,8,128]{4,2,3,1,0:T(4,128)(2,1)S(1)} collective-permute-done((bf16[1,16,4,8,128]{4,2,3,1,0:T(4,128)(2,1)S(1)}, bf16[1,16,4,8,128]{4,2,3,1,0:T(4,128)(2,1)S(1)}, u32[]{:S(2)}, u32[]{:S(2)}) %collective-permute-start.2) | collective-permute-done | bytes 131104 | tf_op jit(solution)/shard_map/ppermute | solution.py:20
  90.1 4.7 %collective-permute-start.5 = (bf16[1,16,4,8,128]{4,2,3,1,0:T(4,128)(2,1)S(1)}, bf16[1,16,4,8,128]{4,2,3,1,0:T(4,128)(2,1)S(1)}, u32[]{:S(2)}, u32[]{:S(2)}) collective-permute-start(bf16[1,16,4,8,128]{4,2,3,1,0:T(4,128)(2,1)S(1)} %collective-permute-done.3), channel_id=1, source_target_pairs={{0,7},{1,0},{2,1},{3,2},{4,3},{5,4},{6,5},{7,6},{8,15},{9,8},{10,9... | collective-permute-start | bytes 393224 | tf_op jit(solution)/shard_map/ppermute | solution.py:23
  94.8 0.1 copy_dynamic-update-slice_fusion.4
  94.9 0.1 copy_dynamic-update-slice_fusion.3
  95.0 2.9 %collective-permute-done.4 = bf16[1,16,4,8,128]{4,2,3,1,0:T(4,128)(2,1)S(1)} collective-permute-done((bf16[1,16,4,8,128]{4,2,3,1,0:T(4,128)(2,1)S(1)}, bf16[1,16,4,8,128]{4,2,3,1,0:T(4,128)(2,1)S(1)}, u32[]{:S(2)}, u32[]{:S(2)}) %collective-permute-start.4) | collective-permute-done | bytes 131104 | tf_op jit(solution)/shard_map/ppermute | solution.py:20
  98.0 0.1 copy_dynamic-update-slice_fusion.1
  98.0 7.5 %collective-permute-done.6 = bf16[1,16,4,8,128]{4,2,3,1,0:T(4,128)(2,1)S(1)} collective-permute-done((bf16[1,16,4,8,128]{4,2,3,1,0:T(4,128)(2,1)S(1)}, bf16[1,16,4,8,128]{4,2,3,1,0:T(4,128)(2,1)S(1)}, u32[]{:S(2)}, u32[]{:S(2)}) %collective-permute-start.6) | collective-permute-done | bytes 131104 | tf_op jit(solution)/shard_map/ppermute | solution.py:20
  105.6 2.9 %fusion.7 = f32[16,8,128,128,1]{3,2,1,0,4:T(8,128)S(1)} fusion(bf16[8,16,4,8,128]{4,2,1,3,0:T(4,128)(2,1)S(1)} %copy_dynamic-update-slice_fusion, f32[128]{0:T(128)S(1)} %iota_convert_fusion, f32[8,16,8,4]{3,1,2,0:T(8,128)S(1)} %copy.38), kind=kOutput, calls=%fused_computation.10 | convolution fusion | flops 134742016 | bytes 9454080 | tf_op jit(solution)/shard_map/nabkr,nakbc->arbc/dot_general | solution.py:60
  108.6 9.4 %multiply_bitcast_fusion = f32[16,128,8,128]{1,3,2,0:T(8,128)} fusion(f32[128]{0:T(128)S(1)} %iota_convert_fusion, f32[128]{0:T(128)S(1)} %get-tuple-element.13, f32[128]{0:T(128)S(1)} %get-tuple-element.12, f32[16,8,128,128,1]{3,2,1,0,4:T(8,128)S(1)} %fusion.7), kind=kOutput, calls=%fused_computation.8 | convolution fusion | flops 3225468928 | bytes 16778752 | tf_op jit(solution)/shard_map/rj,arbc->ajbc/dot_general | solution.py:66
  118.0 9.3 %copy.40 = f32[16,128,8,128]{3,2,1,0:T(8,128)} copy(f32[16,128,8,128]{1,3,2,0:T(8,128)} %multiply_bitcast_fusion) | data formatting | bytes 16777216 | tf_op jit(solution)/shard_map/mul | solution.py:65
  127.2 6.9 %fusion = bf16[2048,1024]{1,0:T(8,128)(2,1)S(1)} fusion(f32[256,8,8,128]{3,2,1,0:T(8,128)} %bitcast.51, bf16[2048,1024]{1,0:T(8,128)(2,1)} %param.7), kind=kLoop, calls=%fused_computation.1 | loop fusion | flops 6291456 | bytes 16777216 | tf_op jit(solution)/shard_map/convert_element_type | solution.py:69
  134.2 2.0 %copy-done = bf16[2048,1024]{1,0:T(8,128)(2,1)} copy-done((bf16[2048,1024]{1,0:T(8,128)(2,1)}, bf16[2048,1024]{1,0:T(8,128)(2,1)S(1)}, u32[]{:S(2)}) %copy-start) | copy-done | bytes 4194328
  136.2 5.8 %convolution_convert_fusion = bf16[1024,1024]{1,0:T(8,128)(2,1)} fusion(bf16[2048,1024]{1,0:T(8,128)(2,1)S(1)} %fusion, bf16[1024,2048]{1,0:T(8,128)(2,1)S(1)} %copy-done.2), kind=kOutput, calls=%fused_computation.12 | convolution fusion | flops 4296015872 | bytes 10485760 | tf_op jit(solution)/shard_map/dot_general | solution.py:71
  142.0 16.6 %fusion.2 = bf16[16,128,8,128]{1,3,2,0:T(8,128)(2,1)} fusion(f32[16,128,8,128]{1,3,2,0:T(8,128)} %copy.27, f32[16,4,8,128]{3,1,2,0:T(4,128)S(1)} %convolution_bitcast_fusion, f32[16,8,4,128]{3,2,1,0:T(4,128)S(1)} %fusion.11), kind=kOutput, calls=%fused_computation.5 | convolution fusion | flops 104857600 | bytes 13107200 | tf_op jit(solution)/shard_map/abkr,akbc->arbc/dot_general | solution.py:51
  158.6 6.7 %copy.28 = bf16[16,128,8,128]{3,2,1,0:T(8,128)(2,1)} copy(bf16[16,128,8,128]{1,3,2,0:T(8,128)(2,1)} %fusion.2) | data formatting | bytes 8388608 | tf_op jit(solution)/shard_map/convert_element_type | solution.py:52
  165.3 7.3 %convert_element_type.90 = bf16[1,2048,1024]{2,1,0:T(8,128)(2,1)} reshape(bf16[16,128,8,128]{3,2,1,0:T(8,128)(2,1)} %copy.28) | data formatting | bytes 8388608 | tf_op jit(solution)/shard_map/convert_element_type | solution.py:52
  172.6 1.1 fusion.10
  173.7 1.0 copy.41
  (23 shorter events, 0.5 us)
Async XLA Ops:
  7.2 165.4 %reduce-scatter.2.cloned.1.call-start = ((), (), s32[]{:S(2)}) async-start(), calls=%async_computation.1 | async-start | bytes 2621440 | tf_op jit(solution)/shard_map/reduce_scatter | solution.py:70
  28.2 22.2 %copy-start.1 = (s32[1,16,8,4]{1,3,2,0:T(4,128)S(1)}, s32[1,16,8,4]{1,3,2,0:T(4,128)}, u32[]{:S(2)}) copy-start(s32[1,16,8,4]{1,3,2,0:T(4,128)} %param.9) | copy-start | bytes 6148
  44.3 37.7 %collective-permute-start = (bf16[1,16,4,8,128]{4,2,3,1,0:T(4,128)(2,1)S(1)}, bf16[1,16,4,8,128]{4,2,3,1,0:T(4,128)(2,1)S(1)}, u32[]{:S(2)}, u32[]{:S(2)}) collective-permute-start(bf16[1,16,4,8,128]{4,2,3,1,0:T(4,128)(2,1)S(1)} %convert_bitcast_fusion), channel_id=1, source_target_pairs={{0,1},{1,2},{2,3},{3,4},{4,5},{5,6},{6,7},{7,0},{8,9},{9,10},{10,1... | collective-permute-start | bytes 393224 | tf_op jit(solution)/shard_map/ppermute | solution.py:20
  47.3 34.7 %collective-permute-start.1 = (bf16[1,16,4,8,128]{4,2,3,1,0:T(4,128)(2,1)S(1)}, bf16[1,16,4,8,128]{4,2,3,1,0:T(4,128)(2,1)S(1)}, u32[]{:S(2)}, u32[]{:S(2)}) collective-permute-start(bf16[1,16,4,8,128]{4,2,3,1,0:T(4,128)(2,1)S(1)} %convert_bitcast_fusion), channel_id=1, source_target_pairs={{0,7},{1,0},{2,1},{3,2},{4,3},{5,4},{6,5},{7,6},{8,15},{9,8},{10,9... | collective-permute-start | bytes 393224 | tf_op jit(solution)/shard_map/ppermute | solution.py:23
  82.0 8.1 %collective-permute-start.2 = (bf16[1,16,4,8,128]{4,2,3,1,0:T(4,128)(2,1)S(1)}, bf16[1,16,4,8,128]{4,2,3,1,0:T(4,128)(2,1)S(1)}, u32[]{:S(2)}, u32[]{:S(2)}) collective-permute-start(bf16[1,16,4,8,128]{4,2,3,1,0:T(4,128)(2,1)S(1)} %collective-permute-done), channel_id=1, source_target_pairs={{0,1},{1,2},{2,3},{3,4},{4,5},{5,6},{6,7},{7,0},{8,9},{9,10},{10,1... | collective-permute-start | bytes 393224 | tf_op jit(solution)/shard_map/ppermute | solution.py:20
  82.1 8.1 %collective-permute-start.3 = (bf16[1,16,4,8,128]{4,2,3,1,0:T(4,128)(2,1)S(1)}, bf16[1,16,4,8,128]{4,2,3,1,0:T(4,128)(2,1)S(1)}, u32[]{:S(2)}, u32[]{:S(2)}) collective-permute-start(bf16[1,16,4,8,128]{4,2,3,1,0:T(4,128)(2,1)S(1)} %collective-permute-done.1), channel_id=1, source_target_pairs={{0,7},{1,0},{2,1},{3,2},{4,3},{5,4},{6,5},{7,6},{8,15},{9,8},{10,9... | collective-permute-start | bytes 393224 | tf_op jit(solution)/shard_map/ppermute | solution.py:23
  90.1 7.8 %collective-permute-start.4 = (bf16[1,16,4,8,128]{4,2,3,1,0:T(4,128)(2,1)S(1)}, bf16[1,16,4,8,128]{4,2,3,1,0:T(4,128)(2,1)S(1)}, u32[]{:S(2)}, u32[]{:S(2)}) collective-permute-start(bf16[1,16,4,8,128]{4,2,3,1,0:T(4,128)(2,1)S(1)} %collective-permute-done.2), channel_id=1, source_target_pairs={{0,1},{1,2},{2,3},{3,4},{4,5},{5,6},{6,7},{7,0},{8,9},{9,10},{10,1... | collective-permute-start | bytes 393224 | tf_op jit(solution)/shard_map/ppermute | solution.py:20
  90.1 7.8 %collective-permute-start.5 = (bf16[1,16,4,8,128]{4,2,3,1,0:T(4,128)(2,1)S(1)}, bf16[1,16,4,8,128]{4,2,3,1,0:T(4,128)(2,1)S(1)}, u32[]{:S(2)}, u32[]{:S(2)}) collective-permute-start(bf16[1,16,4,8,128]{4,2,3,1,0:T(4,128)(2,1)S(1)} %collective-permute-done.3), channel_id=1, source_target_pairs={{0,7},{1,0},{2,1},{3,2},{4,3},{5,4},{6,5},{7,6},{8,15},{9,8},{10,9... | collective-permute-start | bytes 393224 | tf_op jit(solution)/shard_map/ppermute | solution.py:23
  97.9 7.7 %collective-permute-start.6 = (bf16[1,16,4,8,128]{4,2,3,1,0:T(4,128)(2,1)S(1)}, bf16[1,16,4,8,128]{4,2,3,1,0:T(4,128)(2,1)S(1)}, u32[]{:S(2)}, u32[]{:S(2)}) collective-permute-start(bf16[1,16,4,8,128]{4,2,3,1,0:T(4,128)(2,1)S(1)} %collective-permute-done.4), channel_id=1, source_target_pairs={{0,1},{1,2},{2,3},{3,4},{4,5},{5,6},{6,7},{7,0},{8,9},{9,10},{10,1... | collective-permute-start | bytes 393224 | tf_op jit(solution)/shard_map/ppermute | solution.py:20
  127.2 9.0 %copy-start.2 = (bf16[1024,2048]{1,0:T(8,128)(2,1)S(1)}, bf16[1024,2048]{1,0:T(8,128)(2,1)}, u32[]{:S(2)}) copy-start(bf16[1024,2048]{1,0:T(8,128)(2,1)} %param.8) | copy-start | bytes 12582916
  134.2 2.0 %copy-start = (bf16[2048,1024]{1,0:T(8,128)(2,1)}, bf16[2048,1024]{1,0:T(8,128)(2,1)S(1)}, u32[]{:S(2)}) copy-start(bf16[2048,1024]{1,0:T(8,128)(2,1)S(1)} %fusion) | copy-start | bytes 12582916
Sparse Core Ops, SparseCore 0:
  142.1 28.6 reduce-scatter.1
